TPU v7x, 1024 devices: a whole 4x4x32 slice. The times are simulated.
1024 devices in a mesh: dp: 16 (over y, z_hi), seq: 8 (over z_lo), expert: 8 (over x, core).
Axes of the slice: x: 4, y: 4, z: 32 (z_hi: 4, z_lo: 8; z = z_hi * 8 + z_lo), core: 2. Of those that a mesh axis runs over, the one named last changes fastest.
Arguments:
- acts: bfloat16 [16384, 3072], P(('dp', 'seq')), parts along dimension 0, may hold values from -6 to 6
- tangents: bfloat16 [16384, 3072], P(('dp', 'seq')), parts along dimension 0, may hold values from -6 to 6
- cotangents: bfloat16 [16384, 3072], P(('dp', 'seq')), parts along dimension 0, may hold values from -6 to 6
- routes: int32 [16384, 2], P(('dp', 'seq')), parts along dimension 0, may hold values from 0 to 7, all different within a row; in each aligned block of 128 rows (0 to 127, 128 to 255, ...) at most 34 rows name the same one
- gates: float32 [16384, 2], P(('dp', 'seq')), parts along dimension 0, may hold values from 0.1 to 1
- w_in: bfloat16 [8, 3072, 4096], P('expert', None, 'seq'), may hold values from -0.109375 to 0.109375
- w_out: bfloat16 [8, 4096, 3072], P('expert', 'seq'), may hold values from -0.09375 to 0.09375
Outputs:
- tan_out: bfloat16 [16384, 3072], P(('dp', 'seq'), 'expert'), parts along dimension 0
- grad_in: bfloat16 [16384, 3072], P(('dp', 'seq'), 'expert'), parts along dimension 0
There are 16 independent parts, one for each index of `dp`. A program takes and returns all parts, laid end to end along the dimension named above; an argument that names none is the same for every part. Nothing has to cross between parts.
Inputs may be any that keep to these rules, and one draw needn't show every extreme that they name: `routes`: each row names two different experts; in each aligned block of 128 rows (the rows of one index of seq) no expert is named by more than 34 rows, and some expert reaches 34 in some block.
All inputs are finite; a program needn't handle non-finite values.
Results may differ from a plain program's by a relative error of at most 0.02.
Values may be sent and summed in bfloat16 or wider, within the bound.
A program may use at most 64 MiB of HBM per device.

v0:
```python
import jax
import jax.numpy as jnp
from jax import lax
from jax.sharding import PartitionSpec as P


def round_keep(value):
    low = lax.optimization_barrier(value.astype(jnp.bfloat16))
    return low.astype(jnp.float32)


def shards(acts, tangents, cotangents, routes, gates, w_in, w_out):
    rows = acts.shape[0]
    count = lax.axis_size("expert")
    cap = min(rows, 2 * rows // count + 2)
    owner = lax.axis_index("expert")
    onehot = (routes[:, :, None] == jnp.arange(count, dtype=jnp.int32)[None, None, :]).astype(
        jnp.int32
    )
    flat = onehot.reshape(rows * 2, count)
    before = jnp.cumsum(flat, axis=0) - flat
    slot = jnp.sum(before * flat, axis=1).reshape(rows, 2)
    target = routes * cap + slot
    places = jnp.arange(count * cap, dtype=jnp.int32)
    hits = target[:, :, None] == places[None, None, :]
    weight_table = jnp.sum(jnp.where(hits, gates[:, :, None], 0.0), axis=1)
    picked = jnp.any(hits, axis=1).astype(jnp.bfloat16)
    own_pick = lax.dynamic_slice_in_dim(picked, owner * cap, cap, 1)
    stacked = jnp.stack([acts, tangents, cotangents], axis=1)
    buffer = jnp.einsum(
        "rc,rsd->csd", own_pick, stacked, preferred_element_type=jnp.float32
    ).astype(jnp.bfloat16)
    w_first = w_in[0]
    w_second = w_out[0]
    gathered_rows = lax.all_gather(buffer, "seq", axis=0, tiled=True)
    forward = jnp.einsum(
        "nsd,df->nsf", gathered_rows[:, 0:2], w_first, preferred_element_type=jnp.float32
    )
    hidden = forward[:, 0]
    moved = forward[:, 1]
    back = jnp.einsum(
        "nd,fd->nf", gathered_rows[:, 2], w_second, preferred_element_type=jnp.float32
    )
    sig = jax.nn.sigmoid(hidden)
    first = (sig * (1.0 + hidden * (1.0 - sig)) * moved).astype(jnp.bfloat16)
    second = (sig * (1.0 - sig) * (2.0 + hidden * (1.0 - 2.0 * sig)) * moved * back).astype(
        jnp.bfloat16
    )
    part_tan = jnp.dot(first, w_second, preferred_element_type=jnp.float32)
    part_grad = jnp.einsum("nf,df->nd", second, w_first, preferred_element_type=jnp.float32)
    partials = round_keep(jnp.stack([part_tan, part_grad], axis=1))
    values = lax.psum_scatter(partials.astype(jnp.bfloat16), "seq", scatter_dimension=0, tiled=True)
    own_weights = lax.dynamic_slice_in_dim(weight_table, owner * cap, cap, 1)
    term = jnp.einsum(
        "rc,csd->rsd", own_weights, values.astype(jnp.float32), precision=lax.Precision.HIGHEST
    )
    total = lax.psum_scatter(term.astype(jnp.bfloat16), "expert", scatter_dimension=2, tiled=True)
    return (total[:, 0], total[:, 1])


def solution(mesh):
    placed = (
        P(("dp", "seq"), None),
        P(("dp", "seq"), None),
        P(("dp", "seq"), None),
        P(("dp", "seq"), None),
        P(("dp", "seq"), None),
        P("expert", None, "seq"),
        P("expert", "seq", None),
    )
    return jax.shard_map(
        shards,
        mesh=mesh,
        in_specs=placed,
        out_specs=(P(("dp", "seq"), "expert"), P(("dp", "seq"), "expert")),
        check_vma=False,
    )
```

profile of v0, /device:TPU:1, one launch (start us, length us, event | category | flops | bytes accessed | tf_op | source)
XLA Modules:
  0.0 467.8 jit_solution(898553561718422934)
XLA Ops:
  7.2 0.9 copy.45
  10.4 2.1 convolution_convert_fusion.3
  12.4 1.4 copy.48
  13.9 168.9 %all-gather.2.cloned.1.call-done = bf16[272,3,3072]{2,1,0:T(4,128)(2,1)} async-done(((bf16[34,3,3072]{2,1,0:T(4,128)(2,1)}), bf16[272,3,3072]{2,1,0:T(4,128)(2,1)}) %all-gather.2.cloned.1.call-update) | async-done | bytes 5013520 | tf_op jit(solution)/shard_map/all_gather | solution.py:35
  182.9 2.9 slice-done
  185.8 1.9 fusion.2
  187.7 1.1 copy-done.4
  188.8 2.3 fusion
  191.1 1.2 copy-done.1
  192.3 5.1 %slice.36 = bf16[272,1,3072]{2,1,0:T(2,128)(2,1)} slice(bf16[272,3,3072]{2,1,0:T(4,128)(2,1)S(1)} %copy-done.1), slice={[0:272], [2:3], [0:3072]} | slice | bytes 3342336 | tf_op jit(solution)/shard_map/slice | solution.py:42
  197.4 6.6 %fusion.1 = bf16[272,1,3072]{2,0,1:T(8,128)(2,1)} fusion(bf16[1,3072,512]{2,1,0:T(8,128)(2,1)} %param.12, bf16[1,512,3072]{2,1,0:T(8,128)(2,1)S(1)} %copy-done, bf16[272,1,3072]{2,1,0:T(2,128)(2,1)} %slice.36, f32[272,2,512]{2,0,1:T(8,128)} %copy-done.4), kind=kOutput, calls=%fused_computation.4 | convolution fusion | flops 1713922048 | bytes 10747904 | tf_op jit(solution)/shard_map/nf,df->nd/dot_general | solution.py:50
  204.0 2.3 pad_maximum_fusion
  206.2 5.2 %copy.51 = bf16[272,2,3072]{2,1,0:T(2,128)(2,1)} copy(bf16[272,2,3072]{2,0,1:T(8,128)(2,1)S(1)} %pad_maximum_fusion) | data formatting | bytes 6684672 | tf_op jit(solution)/shard_map/optimization_barrier | solution.py:8
  211.7 1.3 dynamic-slice
  213.6 186.5 %all-reduce.3.cloned.1.call-done = bf16[272,2,3072]{2,1,0:T(2,128)(2,1)} async-done(((bf16[272,2,3072]{2,1,0:T(2,128)(2,1)}), bf16[272,2,3072]{2,1,0:T(2,128)(2,1)}) %all-reduce.3.cloned.1.call-update) | async-done | bytes 3342352
  400.1 1.3 constant_dynamic-slice_fusion
  401.4 2.6 convolution_convert_fusion.2
  404.0 4.9 %copy.53 = bf16[128,2,3072]{0,1,2:T(2,128)(2,1)} copy(bf16[128,2,3072]{2,0,1:T(8,128)(2,1)} %convolution_convert_fusion.2) | data formatting | bytes 3145728
  408.9 2.8 copy.73
  411.7 45.2 %reduce-scatter.4.cloned.1.call-done = bf16[384,256]{1,0:T(8,128)(2,1)} async-done(((bf16[3072,256]{1,0:T(8,128)(2,1)}), bf16[384,256]{1,0:T(8,128)(2,1)}) %reduce-scatter.4.cloned.1.call-update) | async-done | bytes 196624
  456.9 1.0 reshape.34
  457.9 0.9 fusion.54
  458.8 1.7 copy.57
  460.5 0.8 copy.58
  (28 shorter events, 2.6 us)
Async XLA Ops:
  7.2 181.6 %copy-start = (bf16[1,512,3072]{2,1,0:T(8,128)(2,1)S(1)}, bf16[1,512,3072]{2,1,0:T(8,128)(2,1)}, u32[]{:S(2)}) copy-start(bf16[1,512,3072]{2,1,0:T(8,128)(2,1)} %param.13) | copy-start | bytes 9437188
  7.2 175.7 %all-gather.2.cloned.1.call-start = ((), (), s32[]{:S(2)}) async-start(), calls=%async_computation.1 | async-start | bytes 7520256 | tf_op jit(solution)/shard_map/all_gather | solution.py:35
  13.9 386.2 %all-reduce.3.cloned.1.call-start = ((), (), s32[]{:S(2)}) async-start(), calls=%async_computation.3 | async-start | bytes 6684672
  182.9 2.9 slice-start
  182.9 2.9 copy-start.3
  187.7 1.1 copy-start.4
  188.8 3.5 copy-start.1
  211.4 2.2 copy-start.2
  211.4 245.4 %reduce-scatter.4.cloned.1.call-start = ((), (), s32[]{:S(2)}) async-start(), calls=%async_computation.2 | async-start | bytes 1769472
Sparse Core Ops, SparseCore 0:
  14.0 168.8 all-gather.1
  211.6 188.5 all-reduce.2
  411.8 45.0 reduce-scatter.3
where the time goes:
time: 468 us
  waiting for transfers between devices  401 us (86%)
  local copies, waits for them, and re-layouts  33.1 us (7%)
  matrix products  15.5 us (3%)
  between operations  14.5 us (3%)
    unnamed x5, waiting for transfers between devices  232 us
    all_gather x1, waiting for transfers between devices, shards(): gathered_rows = lax.all_gather(buffer, 'seq', axis=0, tiled=True)  169 us
    unnamed x18, local copies, waits for them, and re-layouts  16.9 us
  transfers between devices with their start and end apart: 3, of which 3 were waited for; matrix products, arithmetic and copies ran while one was open for 0% of the time, Pallas kernels for 0%

commit v1 on v0

v1 whole, which is shorter than its diff:
```python
import functools

import jax
import jax.numpy as jnp
from jax import lax
from jax.experimental import pallas as pl
from jax.experimental.pallas import tpu as pltpu
from jax.sharding import PartitionSpec as P

MESH = pl.DeviceIdType.MESH
E = 8
N = 8
CAP = 34
MAIN = 32
Z_RUNS = 4
POS = {0: 0, 1: 1, 2: 2, 5: 3, 6: 4, 3: 5, 7: 6, 4: 7}
EARLY = 5


def dot(a, b, dims=((1,), (0,))):
    return lax.dot_general(a, b, (dims, ((), ())), preferred_element_type=jnp.float32)


NT = ((1,), (1,))
TN = ((0,), (0,))


def kernel(
    runs, routes_ref, gates_ref, acts_ref, tangents_ref, cotangents_ref, w_in_hbm, w_out_hbm,
    tan_ref, grad_ref,
    w_in, w_out, rows, extra, mid, part, part_extra, back, back_extra, slots, final,
    w_sems, gather_send, gather_recv, reduce_send, reduce_recv, swap_send, swap_recv,
):
    dp = lax.axis_index("dp")
    seq = lax.axis_index("seq")
    me = lax.axis_index("expert")
    width = acts_ref.shape[1]
    piece = width // E
    toks = acts_ref.shape[0]
    bf16, f32 = jnp.bfloat16, jnp.float32

    load_in = pltpu.make_async_copy(w_in_hbm.at[0], w_in, w_sems.at[0])
    load_out = pltpu.make_async_copy(w_out_hbm.at[0], w_out, w_sems.at[1])
    load_in.start()
    load_out.start()

    ring = runs * N
    place = (dp % runs) * N + seq
    column = dp - dp % runs
    step = 1 - 2 * (me % 2)

    def at(offset):
        there = (place + offset * step + ring) % ring
        return (column + there // N, there % N, me)

    ahead, behind = at(1), at(-1)
    others = [(dp, seq, (me + i) % E) for i in range(1, E)]

    barrier = pltpu.get_barrier_semaphore()
    for device in [ahead, behind] + others:
        pl.semaphore_signal(barrier, inc=1, device_id=device, device_id_type=MESH)

    routes = routes_ref[...]
    experts = lax.broadcasted_iota(jnp.int32, (E, toks), 0)
    first_hit = routes[0:1, :] == experts
    second_hit = routes[1:2, :] == experts
    named = jnp.where(first_hit | second_hit, 1.0, 0.0)
    earlier = jnp.where(
        lax.broadcasted_iota(jnp.int32, (toks, toks), 0) < lax.broadcasted_iota(jnp.int32, (toks, toks), 1), 1.0, 0.0
    ).astype(bf16)
    count = dot(named.astype(bf16), earlier)
    slot_all = jnp.where(named > 0.5, count, -1.0).astype(jnp.int32)
    own_row = experts == me
    slot = jnp.sum(jnp.where(own_row, slot_all, 0), axis=0, keepdims=True)
    gate = jnp.sum(
        jnp.where(own_row & first_hit, gates_ref[0:1, :], 0.0)
        + jnp.where(own_row & second_hit, gates_ref[1:2, :], 0.0),
        axis=0, keepdims=True,
    )
    hits = lax.broadcasted_iota(jnp.int32, (48, toks), 0) == slot
    pick = jnp.where(hits[0:MAIN], 1.0, 0.0).astype(bf16)
    slot_gate = jnp.sum(jnp.where(hits, gate, 0.0), axis=1, keepdims=True)
    pack_row = lax.broadcasted_iota(jnp.int32, (16, toks), 0)
    pack_hit = jnp.where(slot == MAIN + pack_row % 2, 1.0, 0.0)

    sources = (acts_ref, tangents_ref, cotangents_ref)
    for a, source in enumerate(sources):
        rows[a, 0:MAIN, :] = dot(pick, source[...]).astype(bf16)
        packed = jnp.zeros((16, piece), f32)
        for j in range(E):
            chosen = jnp.where(pack_row // 2 == j, pack_hit, 0.0).astype(bf16)
            packed = packed + dot(chosen, source[:, j * piece:(j + 1) * piece])
        extra[0:16, a * piece:(a + 1) * piece] = packed.astype(bf16)

    pl.semaphore_wait(barrier, len(others) + 2)

    def main_rows(k):
        return pl.ds(POS[k] * MAIN, MAIN)

    def gather_copy(k_from, k_to, c, device):
        if c < 3:
            src, dst = rows.at[c, main_rows(k_from), :], rows.at[c, main_rows(k_to), :]
        else:
            src, dst = extra.at[pl.ds(16 * k_from, 16), :], extra.at[pl.ds(16 * k_to, 16), :]
        return pltpu.make_async_remote_copy(
            src_ref=src, dst_ref=dst, send_sem=gather_send.at[k_to, c], recv_sem=gather_recv.at[k_to, c],
            device_id=device, device_id_type=MESH,
        )

    sent = []

    def forward(k_from, k_to, c, device):
        copy = gather_copy(k_from, k_to, c, device)
        copy.start()
        sent.append(copy)

    parts = (3, 0, 1, 2)

    def arrived(k, c):
        gather_copy(k, k, c, ahead).wait_recv()

    for c in parts:
        forward(0, 1, c, ahead)
        forward(0, 5, c, behind)
    for hop in (1, 2):
        for c in parts:
            arrived(hop, c)
            forward(hop, hop + 1, c, ahead)
            arrived(hop + 4, c)
            forward(hop + 4, hop + 5, c, behind)

    def compute(start, size):
        def hidden_tile(i, carry):
            f = pl.ds(pl.multiple_of(i * 256, 256), 256)
            both = dot(rows[0:2, start:start + size, :].reshape(2 * size, width), w_in[:, f])
            h, u = both[0:size], both[size:2 * size]
            p = dot(rows[2, start:start + size, :], w_out[f, :], NT)
            s = jax.nn.sigmoid(h)
            mid[0, start:start + size, f] = (s * (1.0 + h * (1.0 - s)) * u).astype(bf16)
            mid[1, start:start + size, f] = (
                s * (1.0 - s) * (2.0 + h * (1.0 - 2.0 * s)) * u * p
            ).astype(bf16)
            return carry

        lax.fori_loop(0, w_in.shape[1] // 256, hidden_tile, 0)

        def out_tile(i, carry):
            d = pl.ds(pl.multiple_of(i * 256, 256), 256)
            part[0, start:start + size, d] = dot(mid[0, start:start + size, :], w_out[:, d]).astype(bf16)
            part[1, start:start + size, d] = dot(mid[1, start:start + size, :], w_in[d, :], NT).astype(bf16)
            return carry

        lax.fori_loop(0, width // 256, out_tile, 0)

    load_in.wait()
    load_out.wait()
    compute(0, EARLY * MAIN)
    for c in parts:
        arrived(3, c)
        forward(3, 4, c, ahead)
    for c in parts:
        arrived(7, c)
    arrived(4, 3)

    at_row = lax.broadcasted_iota(jnp.int32, (128, 128), 0)
    at_col = lax.broadcasted_iota(jnp.int32, (128, 128), 1)
    turn = (at_row // 16) == (at_col % 16) // 2
    turn = turn & ((at_row % 16) // 2 == at_col // 16) & (at_row % 2 == at_col % 2)
    turn = jnp.where(turn, 1.0, 0.0).astype(bf16)
    late = N * MAIN
    for a in range(3):
        turned = dot(turn, extra[:, a * piece:(a + 1) * piece]).astype(bf16)
        for j in range(E):
            rows[a, late:late + 16, j * piece:(j + 1) * piece] = turned[j * 16:(j + 1) * 16]
    for c in (0, 1, 2):
        arrived(4, c)
    compute(EARLY * MAIN, (N - EARLY) * MAIN + 16)

    for a in range(2):
        spread = jnp.concatenate(
            [part[a, late:late + 16, j * piece:(j + 1) * piece] for j in range(E)], axis=0
        )
        part_extra[:, a * piece:(a + 1) * piece] = dot(turn, spread).astype(bf16)

    def landing(k_from):
        return {4: 3, 3: 2, 2: 1, 1: 0, 7: 5, 6: 4, 5: 6}[k_from]

    def reduce_copy(k_from, c, device):
        slot_at = landing(k_from)
        if c < 2:
            src, dst = part.at[c, main_rows(k_from), :], back.at[slot_at, c]
        else:
            src, dst = part_extra.at[pl.ds(16 * k_from, 16), :], back_extra.at[slot_at]
        return pltpu.make_async_remote_copy(
            src_ref=src, dst_ref=dst, send_sem=reduce_send.at[slot_at, c], recv_sem=reduce_recv.at[slot_at, c],
            device_id=device, device_id_type=MESH,
        )

    def give(k, c, device):
        copy = reduce_copy(k, c, device)
        copy.start()
        sent.append(copy)

    def add(k, k_from, c):
        slot_at = landing(k_from)
        reduce_copy(k_from, c, ahead).wait_recv()
        if c < 2:
            r = main_rows(k)
            part[c, r, :] = (part[c, r, :].astype(f32) + back[slot_at, c].astype(f32)).astype(bf16)
        else:
            r = pl.ds(16 * k, 16)
            part_extra[r, :] = (part_extra[r, :].astype(f32) + back_extra[slot_at].astype(f32)).astype(bf16)

    order = (0, 1, 2)
    for c in order:
        give(4, c, behind)
        give(7, c, ahead)
    for c in order:
        add(3, 4, c)
        give(3, c, behind)
        add(6, 7, c)
        give(6, c, ahead)
    for c in order:
        add(2, 3, c)
        give(2, c, behind)
        add(5, 6, c)
        give(5, c, ahead)
    for c in order:
        add(1, 2, c)
        give(1, c, behind)

    pick_row = lax.broadcasted_iota(jnp.int32, (16, 16), 0)
    pick_col = lax.broadcasted_iota(jnp.int32, (16, 16), 1)
    for c in order:
        reduce_copy(5, c, ahead).wait_recv()
        reduce_copy(1, c, ahead).wait_recv()
        if c < 2:
            total = part[c, 0:MAIN, :].astype(f32) + back[landing(5), c].astype(f32) + back[landing(1), c].astype(f32)
            slots[c, 0:MAIN, :] = (total * slot_gate[0:MAIN]).astype(bf16)
        else:
            total = (
                part_extra[0:16, :].astype(f32)
                + back_extra[landing(5)].astype(f32)
                + back_extra[landing(1)].astype(f32)
            ).astype(bf16)
            for j in range(E):
                select = jnp.where((pick_col == 2 * j + pick_row) & (pick_row < 2), 1.0, 0.0).astype(bf16)
                for a in range(2):
                    value = dot(select, total[:, a * piece:(a + 1) * piece]) * slot_gate[MAIN:48]
                    slots[a, MAIN:48, j * piece:(j + 1) * piece] = value.astype(bf16)

    swaps = []
    for i, device in enumerate(others):
        cols = pl.ds(pl.multiple_of(device[2] * piece, 128), piece)
        copy = pltpu.make_async_remote_copy(
            src_ref=slots.at[:, :, cols], dst_ref=final.at[i + 1],
            send_sem=swap_send.at[i], recv_sem=swap_recv.at[i], device_id=device, device_id_type=MESH,
        )
        copy.start()
        swaps.append(copy)
    final[0] = slots[:, :, pl.ds(pl.multiple_of(me * piece, 128), piece)]

    slot_axis = lax.broadcasted_iota(jnp.int32, (48, toks), 0)
    spreads = []
    for i in range(E):
        sender = (me - i + E) % E
        row = jnp.sum(jnp.where(experts == sender, slot_all, 0), axis=0, keepdims=True)
        spreads.append(jnp.where(slot_axis == row, 1.0, 0.0).astype(bf16))
    spread = jnp.concatenate(spreads, axis=0)
    for copy in swaps:
        copy.wait_recv()
    for a, out in enumerate((tan_ref, grad_ref)):
        out[...] = dot(spread, final[:, a].reshape(E * 48, piece), TN).astype(bf16)
    for copy in sent + swaps:
        copy.wait_send()


def solution(mesh):
    runs = Z_RUNS if mesh.shape["dp"] % Z_RUNS == 0 else 1

    def shards(acts, tangents, cotangents, routes, gates, w_in, w_out):
        toks, width = acts.shape
        hidden = w_in.shape[2]
        piece = width // E
        vmem = pl.BlockSpec(memory_space=pltpu.VMEM)
        hbm = pl.BlockSpec(memory_space=pl.ANY)
        bf16 = jnp.bfloat16
        total = N * MAIN + 16
        return pl.pallas_call(
            functools.partial(kernel, runs),
            out_shape=[jax.ShapeDtypeStruct((toks, piece), bf16)] * 2,
            in_specs=[vmem] * 5 + [hbm] * 2,
            out_specs=[vmem] * 2,
            scratch_shapes=[
                pltpu.VMEM((width, hidden), bf16),
                pltpu.VMEM((hidden, width), bf16),
                pltpu.VMEM((3, total, width), bf16),
                pltpu.VMEM((N * 16, 3 * piece), bf16),
                pltpu.VMEM((2, total, hidden), bf16),
                pltpu.VMEM((2, total, width), bf16),
                pltpu.VMEM((N * 16, 2 * piece), bf16),
                pltpu.VMEM((7, 2, MAIN, width), bf16),
                pltpu.VMEM((7, 16, 2 * piece), bf16),
                pltpu.VMEM((2, 48, width), bf16),
                pltpu.VMEM((E, 2, 48, piece), bf16),
                pltpu.SemaphoreType.DMA((2,)),
                pltpu.SemaphoreType.DMA((N, 4)),
                pltpu.SemaphoreType.DMA((N, 4)),
                pltpu.SemaphoreType.DMA((7, 3)),
                pltpu.SemaphoreType.DMA((7, 3)),
                pltpu.SemaphoreType.DMA((7,)),
                pltpu.SemaphoreType.DMA((7,)),
            ],
            compiler_params=pltpu.CompilerParams(
                collective_id=0, has_side_effects=True, vmem_limit_bytes=48 * 1024 * 1024
            ),
            cost_estimate=pl.CostEstimate(
                flops=10 * total * width * hidden, bytes_accessed=4 * width * hidden, transcendentals=total * hidden
            ),
        )(routes.T, gates.T, acts, tangents, cotangents, w_in, w_out)

    return jax.shard_map(
        shards,
        mesh=mesh,
        in_specs=(
            P(("dp", "seq"), None),
            P(("dp", "seq"), None),
            P(("dp", "seq"), None),
            P(("dp", "seq"), None),
            P(("dp", "seq"), None),
            P("expert", None, "seq"),
            P("expert", "seq", None),
        ),
        out_specs=(P(("dp", "seq"), "expert"), P(("dp", "seq"), "expert")),
        check_vma=False,
    )
```

time: 468 us -> 124 us (0.26)
  waiting for transfers between devices: 401 us -> 0 us
  Pallas kernels: 0 us -> 115 us
  local copies, waits for them, and re-layouts: 33.1 us -> 7.92 us
  matrix products: 15.5 us -> 0 us
  between operations: 14.5 us -> 0.65 us
    unnamed x5 -> x0, waiting for transfers between devices: 232 us -> none
    all_gather x1 -> x0, waiting for transfers between devices: 169 us -> none  [shards(): gathered_rows = lax.all_gather(buffer, 'seq', axis=0, tiled=True)]
    pallas_call x0 -> x1, Pallas kernels: none -> 115 us  [shards(): pl.pallas_call(functools.partial(kernel, runs), out_shape=[jax.ShapeDtype...]
    dot_general x5 -> x0, matrix products: 15.5 us -> none  [the longest x1 6.6 us: shards(): jnp.einsum('nf,df->nd', second, w_first, preferred_element_type=jnp.float32)]
    slice x5 -> x0, local copies, waits for them, and re-layouts: 9.17 us -> none  [the longest x1 5.12 us: shards(): gathered_rows[:, 2]]
    unnamed x18 -> x14, local copies, waits for them, and re-layouts: 16.9 us -> 7.92 us
    optimization_barrier x1 -> x0, local copies, waits for them, and re-layouts: 5.17 us -> none  [round_keep(): low = lax.optimization_barrier(value.astype(jnp.bfloat16))]
  transfers between devices with their start and end apart: 3 -> 0, of which waited for: 3 -> 0; matrix products, arithmetic and copies ran while one was open for 0% -> 0% of each run, Pallas kernels for 0% -> 0%
where the time goes in v1:
time: 124 us
  Pallas kernels  115 us (93%)
  local copies, waits for them, and re-layouts  7.92 us (6%)
    pallas_call x1, Pallas kernels, shards(): pl.pallas_call(functools.partial(kernel, runs), out_shape=[jax.ShapeDtype...  115 us
    unnamed x14, local copies, waits for them, and re-layouts  7.92 us

profile of v1, /device:TPU:1, one launch (start us, length us, event | category | flops | bytes accessed | tf_op | source)
XLA Modules:
  0.0 123.8 jit_solution(4978288351215595575)
XLA Ops:
  0.6 0.0 copy-start
  0.6 1.9 %copy-done = bf16[1,3072,512]{2,1,0:T(8,128)(2,1)S(1)} copy-done((bf16[1,3072,512]{2,1,0:T(8,128)(2,1)S(1)}, bf16[1,3072,512]{2,1,0:T(8,128)(2,1)}, u32[]{:S(2)}) %copy-start) | copy-done | bytes 3145752
  2.5 0.0 copy-start.1
  2.5 1.1 copy-done.1
  3.7 0.0 copy-start.2
  3.7 1.1 copy-done.2
  4.8 0.0 copy-start.3
  4.8 1.1 copy-done.3
  5.9 0.0 copy-start.4
  5.9 0.7 copy-done.4
  6.6 0.0 copy-start.5
  6.6 0.7 copy-done.5
  7.3 115.3 %shard_map.86 = (bf16[128,384]{1,0:T(8,128)(2,1)S(1)}, bf16[128,384]{1,0:T(8,128)(2,1)S(1)}) custom-call(s32[2,128]{1,0:T(2,128)S(1)} %bitcast.2, f32[2,128]{1,0:T(2,128)S(1)} %bitcast.3, bf16[128,3072]{1,0:T(8,128)(2,1)S(1)} %copy-done.1, bf16[128,3072]{1,0:T(8,128)(2,1)S(1)} %copy-done.2, bf16[128,3072]{1,0:T(8,128)(2,1)S(1)} %copy-done.3, ...), custom_call_target="tpu_custom_call" | custom-call | flops 4278190080 | bytes 6291456 | tf_op jit(solution)/shard_map/pallas_call | solution.py:289
  122.6 0.6 copy.11
  123.2 0.6 copy.12
Async XLA Ops:
  0.6 1.9 %copy-start = (bf16[1,3072,512]{2,1,0:T(8,128)(2,1)S(1)}, bf16[1,3072,512]{2,1,0:T(8,128)(2,1)}, u32[]{:S(2)}) copy-start(bf16[1,3072,512]{2,1,0:T(8,128)(2,1)} %w_in_hbm.1) | copy-start | bytes 9437188
  2.5 1.1 copy-start.1
  3.7 1.1 copy-start.2
  4.8 1.1 copy-start.3
  5.9 0.7 copy-start.4
  6.6 0.7 copy-start.5

commit v2 on v0

v2 whole, which is shorter than its diff:
```python
import functools

import jax
import jax.numpy as jnp
from jax import lax
from jax.experimental import pallas as pl
from jax.experimental.pallas import tpu as pltpu
from jax.sharding import PartitionSpec as P

MESH = pl.DeviceIdType.MESH
E = 8
N = 8
MAIN = 32
Z_RUNS = 4
POS = {0: 0, 1: 1, 2: 2, 5: 3, 6: 4, 3: 5, 7: 6, 4: 7}
EARLY = 5 * MAIN
EXTRA = N * MAIN
TOTAL = EXTRA + 16


def dot(a, b, dims=((1,), (0,))):
    return lax.dot_general(a, b, (dims, ((), ())), preferred_element_type=jnp.float32)


NT = ((1,), (1,))
TN = ((0,), (0,))


def main_rows(k):
    return pl.ds(POS[k] * MAIN, MAIN)


def block_of(side, d, i):
    if (side == 0) == (i % 2 == 0):
        return d
    return 4 + d if d <= 3 else None


def kernel(
    runs, routes_hbm, gates_hbm, acts_hbm, tangents_hbm, cotangents_hbm, w_in_hbm, w_out_hbm,
    tan_ref, grad_ref,
    routes_v, gates_v, acts_v, tangents_v, cotangents_v, w_in, w_out, raw_own, raw, metas, stage, tails, tails_out,
    rows, extra, gate_rows, mid, part, part_extra, back, back_extra, land, sums, sums_in, slots, final,
    load_sems, raw_send, raw_recv, meta_send, meta_recv, cot_send, cot_recv, pick_send, pick_recv,
    tail_send, tail_recv, land_send, land_recv, tan_send, tan_recv, sum_send, sum_recv, swap_send, swap_recv,
):
    dp = lax.axis_index("dp")
    seq = lax.axis_index("seq")
    me = lax.axis_index("expert")
    toks, width = acts_hbm.shape
    piece = width // E
    bf16, f32 = jnp.bfloat16, jnp.float32

    def cols(owner):
        return pl.ds(pl.multiple_of(owner * piece, 128), piece)

    loads = [
        pltpu.make_async_copy(src, dst, load_sems.at[n])
        for n, (src, dst) in enumerate((
            (acts_hbm.at[:, cols(me)], raw_own.at[0]),
            (tangents_hbm.at[:, cols(me)], raw_own.at[1]),
            (routes_hbm, routes_v),
            (gates_hbm, gates_v),
            (cotangents_hbm, cotangents_v),
            (acts_hbm, acts_v),
            (tangents_hbm, tangents_v),
            (w_in_hbm.at[0], w_in),
            (w_out_hbm.at[0], w_out),
        ))
    ]
    for load in loads:
        load.start()

    ring = runs * N
    place = (dp % runs) * N + seq
    column = dp - dp % runs
    step = 1 - 2 * (me % 2)

    def at(offset):
        there = (place + offset * step + ring) % ring
        return (column + there // N, there % N, me)

    ahead, behind = at(1), at(-1)
    away = (ahead, behind)
    home = (behind, ahead)
    others = [(dp, seq, (me + i) % E) for i in range(1, E)]

    barrier = pltpu.get_barrier_semaphore()
    for device in [ahead, behind] + others:
        pl.semaphore_signal(barrier, inc=1, device_id=device, device_id_type=MESH)

    sent = []

    def remote(src, dst, send, recv, device):
        return pltpu.make_async_remote_copy(
            src_ref=src, dst_ref=dst, send_sem=send, recv_sem=recv, device_id=device, device_id_type=MESH
        )

    def start(copy):
        copy.start()
        sent.append(copy)

    def raw_copy(side, d):
        src = raw_own if d == 1 else raw.at[side * 4 + d - 2]
        n = side * 4 + d - 1
        return remote(src, raw.at[n], raw_send.at[n], raw_recv.at[n], away[side])

    def meta_copy(side, d):
        n = side * 4 + d
        return remote(
            metas.at[0 if d == 1 else n - 1], metas.at[n], meta_send.at[n - 1], meta_recv.at[n - 1], away[side]
        )

    def cot_copies(side, d):
        k = side * 4 + d
        k_from = 0 if d == 1 else k - 1
        return [
            remote(
                rows.at[2, main_rows(k_from), :], rows.at[2, main_rows(k), :],
                cot_send.at[k, 0], cot_recv.at[k, 0], away[side],
            ),
            remote(
                extra.at[pl.ds(16 * k_from, 16), :], extra.at[pl.ds(16 * k, 16), :],
                cot_send.at[k, 1], cot_recv.at[k, 1], away[side],
            ),
        ]

    loads[0].wait()
    loads[1].wait()
    pl.semaphore_wait(barrier, len(others) + 2)
    for side in (0, 1):
        start(raw_copy(side, 1))

    loads[2].wait()
    loads[3].wait()
    routes = routes_v[...]
    experts = (lax.broadcasted_iota(jnp.int32, (E, toks), 0) + me) % E
    first_hit = routes[0:1, :] == experts
    second_hit = routes[1:2, :] == experts
    named = jnp.where(first_hit | second_hit, 1.0, 0.0)
    earlier = jnp.where(
        lax.broadcasted_iota(jnp.int32, (toks, toks), 0) < lax.broadcasted_iota(jnp.int32, (toks, toks), 1), 1.0, 0.0
    ).astype(bf16)
    slot_all = jnp.where(named > 0.5, dot(named.astype(bf16), earlier), -1.0)
    gate_all = jnp.where(first_hit, gates_v[0:1, :], 0.0) + jnp.where(second_hit, gates_v[1:2, :], 0.0)
    metas[0, 0:E, :] = slot_all
    metas[0, E:2 * E, :] = gate_all
    for side in (0, 1):
        start(meta_copy(side, 1))

    main_iota = lax.broadcasted_iota(jnp.int32, (MAIN, toks), 0).astype(f32)
    tail_row = lax.broadcasted_iota(jnp.int32, (16, toks), 0)
    tail_iota = (MAIN + tail_row % 2).astype(f32)
    tail_block = tail_row // 2

    def hot(slot):
        return jnp.where(main_iota == slot, 1.0, 0.0)

    def tail_hot(slot, k):
        return jnp.where((tail_iota == slot) & (tail_block == k), 1.0, 0.0)

    slot = slot_all[0:1, :]
    pick = hot(slot)
    loads[4].wait()
    packed = jnp.zeros((16, piece), f32)
    for j in range(E):
        chosen = jnp.concatenate([pick, tail_hot(slot, j)], axis=0).astype(bf16)
        got = dot(chosen, cotangents_v[:, j * piece:(j + 1) * piece])
        rows[2, 0:MAIN, j * piece:(j + 1) * piece] = got[0:MAIN].astype(bf16)
        packed = packed + got[MAIN:]
    extra[0:16, :] = packed.astype(bf16)

    chosen = jnp.concatenate([tail_hot(slot_all[i:i + 1, :], 0) for i in range(E)], axis=0).astype(bf16)
    for a in range(2):
        got = dot(chosen, raw_own[a])
        for i in range(E):
            tails[i, a] = got[i * 16:(i + 1) * 16]

    def pick_copy(side, d, i):
        k = block_of(side, d, i)
        b = side * 4 + d - 1
        return remote(
            stage.at[b, i], rows.at[pl.ds(0, 2), main_rows(k), cols(me)],
            pick_send.at[b, i], pick_recv.at[k, i], others[i - 1],
        )

    def pick_arrived(k):
        for i in range(1, E):
            remote(
                stage.at[0, i], rows.at[pl.ds(0, 2), main_rows(k), cols((me - i + E) % E)],
                pick_send.at[0, i], pick_recv.at[k, i], others[i - 1],
            ).wait_recv()

    def pick_rows(side, d):
        b = side * 4 + d - 1
        live = [i for i in range(E) if block_of(side, d, i) is not None]
        slots_of = [metas[b + 1, i:i + 1, :] for i in live]
        chosen = jnp.concatenate(
            [hot(s) for s in slots_of] + [tail_hot(s, block_of(side, d, i)) for i, s in zip(live, slots_of)], axis=0
        ).astype(bf16)
        for a in range(2):
            got = dot(chosen, raw[b, a])
            for n, i in enumerate(live):
                value = got[n * MAIN:(n + 1) * MAIN].astype(bf16)
                if i == 0:
                    rows[a, main_rows(block_of(side, d, 0)), cols(me)] = value
                else:
                    stage[b, i, a] = value
                first = len(live) * MAIN + n * 16
                tails[i, a] = tails[i, a] + got[first:first + 16]
        for i in live:
            if i:
                start(pick_copy(side, d, i))

    for d in (1, 2, 3, 4):
        for side in (0, 1):
            raw_copy(side, d).wait_recv()
            if d < 4:
                start(raw_copy(side, d + 1))
            meta_copy(side, d).wait_recv()
            if d < 4:
                start(meta_copy(side, d + 1))
        for side in (0, 1):
            if d > 1 and (side == 0 or d <= 4):
                for copy in cot_copies(side, d - 1):
                    copy.wait_recv()
            if side == 0 or d < 4:
                for copy in cot_copies(side, d):
                    start(copy)
        if d == 1:
            loads[5].wait()
            loads[6].wait()
            for a, source in enumerate((acts_v, tangents_v)):
                rows[a, 0:MAIN, :] = dot(pick.astype(bf16), source[...]).astype(bf16)
        for side in (0, 1):
            pick_rows(side, d)

    def tail_copy(i):
        return remote(
            tails_out.at[i], rows.at[pl.ds(0, 2), pl.ds(EXTRA, 16), cols(me)],
            tail_send.at[i], tail_recv.at[i], others[i - 1],
        )

    for i in range(E):
        if i:
            tails_out[i] = tails[i].astype(bf16)
            start(tail_copy(i))
        else:
            rows[0:2, EXTRA:TOTAL, cols(me)] = tails[0].astype(bf16)

    tail_gate = jnp.zeros((16, 1), f32)
    for k in range(N):
        slot_k, gate_k = metas[k, 0:1, :], metas[k, E:E + 1, :]
        gate_rows[main_rows(k), :] = jnp.sum(hot(slot_k) * gate_k, axis=1, keepdims=True)
        tail_gate = tail_gate + jnp.sum(tail_hot(slot_k, k) * gate_k, axis=1, keepdims=True)
    gate_rows[EXTRA:TOTAL, :] = tail_gate

    def compute(first_row, size):
        here = slice(first_row, first_row + size)

        def hidden_tile(n, carry):
            f = pl.ds(pl.multiple_of(n * 256, 256), 256)
            both = dot(rows[0:2, here, :].reshape(2 * size, width), w_in[:, f])
            h, u = both[0:size], both[size:2 * size]
            p = dot(rows[2, here, :], w_out[f, :], NT)
            s = jax.nn.sigmoid(h)
            gate = gate_rows[here, :]
            mid[0, here, f] = (s * (1.0 + h * (1.0 - s)) * u * gate).astype(bf16)
            mid[1, here, f] = (s * (1.0 - s) * (2.0 + h * (1.0 - 2.0 * s)) * u * p * gate).astype(bf16)
            return carry

        lax.fori_loop(0, w_in.shape[1] // 256, hidden_tile, 0)

        def out_tile(n, carry):
            d = pl.ds(pl.multiple_of(n * 256, 256), 256)
            part[0, here, d] = dot(mid[0, here, :], w_out[:, d]).astype(bf16)
            part[1, here, d] = dot(mid[1, here, :], w_in[d, :], NT).astype(bf16)
            return carry

        lax.fori_loop(0, width // 256, out_tile, 0)

    loads[7].wait()
    loads[8].wait()
    for k in (1, 2, 5, 6):
        pick_arrived(k)
    compute(0, EARLY)
    for k in (3, 7, 4):
        pick_arrived(k)
    for i in range(1, E):
        remote(
            tails_out.at[i], rows.at[pl.ds(0, 2), pl.ds(EXTRA, 16), cols((me - i + E) % E)],
            tail_send.at[i], tail_recv.at[i], others[i - 1],
        ).wait_recv()
    for copy in cot_copies(0, 4):
        copy.wait_recv()

    at_row = lax.broadcasted_iota(jnp.int32, (128, 128), 0)
    at_col = lax.broadcasted_iota(jnp.int32, (128, 128), 1)
    turn = (at_row // 16) == (at_col % 16) // 2
    turn = turn & ((at_row % 16) // 2 == at_col // 16) & (at_row % 2 == at_col % 2)
    turn = jnp.where(turn, 1.0, 0.0).astype(bf16)
    turned = dot(turn, extra[...]).astype(bf16)
    for j in range(E):
        rows[2, EXTRA:TOTAL, j * piece:(j + 1) * piece] = turned[j * 16:(j + 1) * 16]
    compute(EARLY, TOTAL - EARLY)

    halves = ((EARLY, TOTAL - EARLY), (0, EARLY))

    def land_copy(half, i):
        r = pl.ds(*halves[half])
        return remote(
            part.at[1, r, cols(others[i - 1][2])], land.at[i, r, :],
            land_send.at[half, i], land_recv.at[half, i], others[i - 1],
        )

    landing = {4: 3, 3: 2, 2: 1, 1: 0, 7: 5, 6: 4, 5: 6}

    def tan_copy(k, c):
        n = landing[k]
        device = behind if k <= 4 else ahead
        if c == 0:
            src, dst = part.at[0, main_rows(k), :], back.at[n]
        else:
            src, dst = part_extra.at[pl.ds(16 * k, 16), :], back_extra.at[n]
        return remote(src, dst, tan_send.at[n, c], tan_recv.at[n, c], device)

    def tan_add(k, k_from):
        n = landing[k_from]
        r, x = main_rows(k), pl.ds(16 * k, 16)
        tan_copy(k_from, 0).wait_recv()
        part[0, r, :] = (part[0, r, :].astype(f32) + back[n].astype(f32)).astype(bf16)
        start(tan_copy(k, 0))
        tan_copy(k_from, 1).wait_recv()
        part_extra[x, :] = (part_extra[x, :].astype(f32) + back_extra[n].astype(f32)).astype(bf16)
        start(tan_copy(k, 1))

    for i in range(1, E):
        start(land_copy(0, i))
    start(tan_copy(4, 0))
    start(tan_copy(7, 0))
    spread = jnp.concatenate([part[0, EXTRA:TOTAL, j * piece:(j + 1) * piece] for j in range(E)], axis=0)
    part_extra[...] = dot(turn, spread).astype(bf16)
    start(tan_copy(4, 1))
    start(tan_copy(7, 1))
    for i in range(1, E):
        start(land_copy(1, i))
    land[0] = part[1, :, cols(me)]

    def combine(side, d):
        b = 0 if d == 0 else side * 4 + d
        chosen, values = [], []
        for i in range(E):
            k = 0 if d == 0 else block_of(side, d, i)
            if k is None:
                continue
            s = metas[b, (E - i) % E:(E - i) % E + 1, :]
            chosen += [hot(s), tail_hot(s, k)]
            values += [land[i, main_rows(k), :], land[i, EXTRA:TOTAL, :]]
        return dot(jnp.concatenate(chosen, axis=0).astype(bf16), jnp.concatenate(values, axis=0), TN)

    def sum_copy(side, d):
        n = side * 4 + d - 1
        return remote(sums.at[n], sums_in.at[n], sum_send.at[n], sum_recv.at[n], home[side])

    def sum_step(side, d):
        value = combine(side, d)
        if d < 4:
            sum_copy(side, d + 1).wait_recv()
            value = value + sums_in[side * 4 + d].astype(f32)
        sums[side * 4 + d - 1] = value.astype(bf16)
        start(sum_copy(side, d))

    tan_add(3, 4)
    tan_add(6, 7)
    for i in range(1, E):
        land_copy(0, i).wait_recv()
    sum_step(0, 4)
    sum_step(1, 4)
    tan_add(2, 3)
    tan_add(5, 6)
    sum_step(0, 3)
    sum_step(1, 3)
    tan_add(1, 2)
    for i in range(1, E):
        land_copy(1, i).wait_recv()
    sum_step(0, 2)
    sum_step(1, 2)

    for c in (0, 1):
        tan_copy(5, c).wait_recv()
        tan_copy(1, c).wait_recv()
    n, m = landing[5], landing[1]
    slots[0:MAIN, :] = (part[0, 0:MAIN, :].astype(f32) + back[n].astype(f32) + back[m].astype(f32)).astype(bf16)
    total = part_extra[0:16, :].astype(f32) + back_extra[n].astype(f32) + back_extra[m].astype(f32)
    total = total.astype(bf16)
    pick_row = lax.broadcasted_iota(jnp.int32, (128, 16), 0)
    pick_col = lax.broadcasted_iota(jnp.int32, (128, 16), 1)
    select = (pick_col == 2 * (pick_row // 16) + pick_row % 16) & (pick_row % 16 < 2)
    unpacked = dot(jnp.where(select, 1.0, 0.0).astype(bf16), total).astype(bf16)
    for j in range(E):
        slots[MAIN:48, j * piece:(j + 1) * piece] = unpacked[j * 16:(j + 1) * 16]

    def swap_copy(i):
        return remote(
            slots.at[:, cols(others[i - 1][2])], final.at[i], swap_send.at[i], swap_recv.at[i], others[i - 1]
        )

    for i in range(1, E):
        start(swap_copy(i))
    final[0] = slots[:, cols(me)]
    sum_step(0, 1)
    sum_step(1, 1)
    own = combine(0, 0)

    slot_iota = lax.broadcasted_iota(jnp.int32, (48, toks), 0).astype(f32)
    spread = jnp.concatenate(
        [jnp.where(slot_iota == metas[0, (E - i) % E:(E - i) % E + 1, :], 1.0, 0.0) for i in range(E)], axis=0
    ).astype(bf16)
    for i in range(1, E):
        swap_copy(i).wait_recv()
    tan_ref[...] = dot(spread, final[...].reshape(E * 48, piece), TN).astype(bf16)
    sum_copy(0, 1).wait_recv()
    sum_copy(1, 1).wait_recv()
    grad_ref[...] = (own + sums_in[0].astype(f32) + sums_in[4].astype(f32)).astype(bf16)
    for copy in sent:
        copy.wait_send()


def solution(mesh):
    runs = Z_RUNS if mesh.shape["dp"] % Z_RUNS == 0 else 1

    def shards(acts, tangents, cotangents, routes, gates, w_in, w_out):
        toks, width = acts.shape
        hidden = w_in.shape[2]
        piece = width // E
        vmem = pl.BlockSpec(memory_space=pltpu.VMEM)
        hbm = pl.BlockSpec(memory_space=pl.ANY)
        bf16, f32 = jnp.bfloat16, jnp.float32

        def sems(*shape):
            return [pltpu.SemaphoreType.DMA(shape)] * 2

        return pl.pallas_call(
            functools.partial(kernel, runs),
            out_shape=[jax.ShapeDtypeStruct((toks, piece), bf16)] * 2,
            in_specs=[hbm] * 7,
            out_specs=[vmem] * 2,
            scratch_shapes=[
                pltpu.VMEM((2, toks), jnp.int32),
                pltpu.VMEM((2, toks), f32),
                pltpu.VMEM((toks, width), bf16),
                pltpu.VMEM((toks, width), bf16),
                pltpu.VMEM((toks, width), bf16),
                pltpu.VMEM((width, hidden), bf16),
                pltpu.VMEM((hidden, width), bf16),
                pltpu.VMEM((2, toks, piece), bf16),
                pltpu.VMEM((8, 2, toks, piece), bf16),
                pltpu.VMEM((9, 2 * E, toks), f32),
                pltpu.VMEM((8, E, 2, MAIN, piece), bf16),
                pltpu.VMEM((E, 2, 16, piece), f32),
                pltpu.VMEM((E, 2, 16, piece), bf16),
                pltpu.VMEM((3, TOTAL, width), bf16),
                pltpu.VMEM((N * 16, piece), bf16),
                pltpu.VMEM((TOTAL, 1), f32),
                pltpu.VMEM((2, TOTAL, hidden), bf16),
                pltpu.VMEM((2, TOTAL, width), bf16),
                pltpu.VMEM((N * 16, piece), bf16),
                pltpu.VMEM((7, MAIN, width), bf16),
                pltpu.VMEM((7, 16, piece), bf16),
                pltpu.VMEM((E, TOTAL, piece), bf16),
                pltpu.VMEM((8, toks, piece), bf16),
                pltpu.VMEM((8, toks, piece), bf16),
                pltpu.VMEM((48, width), bf16),
                pltpu.VMEM((E, 48, piece), bf16),
                pltpu.SemaphoreType.DMA((9,)),
            ]
            + sems(8) + sems(8) + sems(8, 2) + sems(8, 8) + sems(8) + sems(2, 8) + sems(7, 2) + sems(8) + sems(8),
            compiler_params=pltpu.CompilerParams(
                collective_id=0, has_side_effects=True, vmem_limit_bytes=60 * 1024 * 1024
            ),
            cost_estimate=pl.CostEstimate(
                flops=10 * TOTAL * width * hidden, bytes_accessed=4 * width * hidden, transcendentals=TOTAL * hidden
            ),
        )(routes.T, gates.T, acts, tangents, cotangents, w_in, w_out)

    return jax.shard_map(
        shards,
        mesh=mesh,
        in_specs=(
            P(("dp", "seq"), None),
            P(("dp", "seq"), None),
            P(("dp", "seq"), None),
            P(("dp", "seq"), None),
            P(("dp", "seq"), None),
            P("expert", None, "seq"),
            P("expert", "seq", None),
        ),
        out_specs=(P(("dp", "seq"), "expert"), P(("dp", "seq"), "expert")),
        check_vma=False,
    )
```

time: 468 us -> 105 us (0.22)
  waiting for transfers between devices: 401 us -> 0 us
  Pallas kernels: 0 us -> 101 us
  local copies, waits for them, and re-layouts: 33.1 us -> 3.09 us
  matrix products: 15.5 us -> 0 us
  between operations: 14.5 us -> 0.64 us
    unnamed x5 -> x0, waiting for transfers between devices: 232 us -> none
    all_gather x1 -> x0, waiting for transfers between devices: 169 us -> none  [shards(): gathered_rows = lax.all_gather(buffer, 'seq', axis=0, tiled=True)]
    pallas_call x0 -> x1, Pallas kernels: none -> 101 us  [shards(): pl.pallas_call(functools.partial(kernel, runs), out_shape=[jax.ShapeDtype...]
    dot_general x5 -> x0, matrix products: 15.5 us -> none  [the longest x1 6.6 us: shards(): jnp.einsum('nf,df->nd', second, w_first, preferred_element_type=jnp.float32)]
    unnamed x18 -> x2, local copies, waits for them, and re-layouts: 16.9 us -> 3.09 us
    slice x5 -> x0, local copies, waits for them, and re-layouts: 9.17 us -> none  [the longest x1 5.12 us: shards(): gathered_rows[:, 2]]
    optimization_barrier x1 -> x0, local copies, waits for them, and re-layouts: 5.17 us -> none  [round_keep(): low = lax.optimization_barrier(value.astype(jnp.bfloat16))]
  transfers between devices with their start and end apart: 3 -> 0, of which waited for: 3 -> 0; matrix products, arithmetic and copies ran while one was open for 0% -> 0% of each run, Pallas kernels for 0% -> 0%
where the time goes in v2:
time: 105 us
  Pallas kernels  101 us (96%)
  local copies, waits for them, and re-layouts  3.09 us (3%)
    pallas_call x1, Pallas kernels, shards(): pl.pallas_call(functools.partial(kernel, runs), out_shape=[jax.ShapeDtype...  101 us
    unnamed x2, local copies, waits for them, and re-layouts  3.09 us

profile of v2, /device:TPU:1, one launch (start us, length us, event | category | flops | bytes accessed | tf_op | source)
XLA Modules:
  0.0 105.0 jit_solution(2628288393586239371)
XLA Ops:
  0.6 101.3 %shard_map.86 = (bf16[128,384]{1,0:T(8,128)(2,1)}, bf16[128,384]{1,0:T(8,128)(2,1)}) custom-call(s32[2,128]{1,0:T(2,128)} %bitcast.2, f32[2,128]{1,0:T(2,128)} %bitcast.3, bf16[128,3072]{1,0:T(8,128)(2,1)} %acts_hbm.1, bf16[128,3072]{1,0:T(8,128)(2,1)} %tangents_hbm.1, bf16[128,3072]{1,0:T(8,128)(2,1)} %cotangents_hbm.1, bf16[1,3072,512]{2,1,0:T(8,128)(2,1)} %w_in_hbm.1, ...), custom_call_target="tpu_custom_call" | custom-call | flops 4278190080 | bytes 6291456 | tf_op jit(solution)/shard_map/pallas_call | solution.py:443
  102.0 1.5 %copy.11 = bf16[128,384]{1,0:T(8,128)(2,1)} copy(bf16[128,384]{1,0:T(8,128)(2,1)} %get-tuple-element.4) | data formatting | bytes 196608
  103.5 1.5 %copy.12 = bf16[128,384]{1,0:T(8,128)(2,1)} copy(bf16[128,384]{1,0:T(8,128)(2,1)} %get-tuple-element.5) | data formatting | bytes 196608

commit v3 on v2

--- a/solution.py
+++ b/solution.py
@@ -68,7 +68,7 @@
             (w_out_hbm.at[0], w_out),
         ))
     ]
-    for load in loads:
+    for load in loads[:5]:
         load.start()
 
     ring = runs * N
@@ -130,6 +130,8 @@
     pl.semaphore_wait(barrier, len(others) + 2)
     for side in (0, 1):
         start(raw_copy(side, 1))
+    loads[5].start()
+    loads[6].start()
 
     loads[2].wait()
     loads[3].wait()
@@ -228,6 +230,8 @@
                 for copy in cot_copies(side, d):
                     start(copy)
         if d == 1:
+            loads[7].start()
+            loads[8].start()
             loads[5].wait()
             loads[6].wait()
             for a, source in enumerate((acts_v, tangents_v)):

time: 105 us -> 105 us (level)
  no operation moved by 1% of the time
where the time goes in v3:
time: 105 us
  Pallas kernels  101 us (96%)
  local copies, waits for them, and re-layouts  3.09 us (3%)
    pallas_call x1, Pallas kernels, shards(): pl.pallas_call(functools.partial(kernel, runs), out_shape=[jax.ShapeDtype...  101 us
    unnamed x2, local copies, waits for them, and re-layouts  3.09 us

profile of v3, /device:TPU:1, one launch (start us, length us, event | category | flops | bytes accessed | tf_op | source)
XLA Modules:
  0.0 105.0 jit_solution(4409570430651875051)
XLA Ops:
  0.6 101.3 %shard_map.86 = (bf16[128,384]{1,0:T(8,128)(2,1)}, bf16[128,384]{1,0:T(8,128)(2,1)}) custom-call(s32[2,128]{1,0:T(2,128)} %bitcast.2, f32[2,128]{1,0:T(2,128)} %bitcast.3, bf16[128,3072]{1,0:T(8,128)(2,1)} %acts_hbm.1, bf16[128,3072]{1,0:T(8,128)(2,1)} %tangents_hbm.1, bf16[128,3072]{1,0:T(8,128)(2,1)} %cotangents_hbm.1, bf16[1,3072,512]{2,1,0:T(8,128)(2,1)} %w_in_hbm.1, ...), custom_call_target="tpu_custom_call" | custom-call | flops 4278190080 | bytes 6291456 | tf_op jit(solution)/shard_map/pallas_call | solution.py:447
  101.9 1.5 %copy.11 = bf16[128,384]{1,0:T(8,128)(2,1)} copy(bf16[128,384]{1,0:T(8,128)(2,1)} %get-tuple-element.4) | data formatting | bytes 196608
  103.5 1.5 %copy.12 = bf16[128,384]{1,0:T(8,128)(2,1)} copy(bf16[128,384]{1,0:T(8,128)(2,1)} %get-tuple-element.5) | data formatting | bytes 196608
